TPU v7x, 32 devices: a whole 2x2x4 slice. The times are simulated.
32 devices in a mesh: dp: 16 (over z, x, core), tensor: 2 (over y).
Axes of the slice: x: 2, y: 2, z: 4, core: 2. Of those that a mesh axis runs over, the one named last changes fastest.
Arguments:
- hidden_in: bfloat16 [4096, 4096], P(('dp', 'tensor')), may hold values from -12 to 12
- norm_gain: bfloat16 [4096], replicated, may hold values from 0.5 to 1.5
- w_query: bfloat16 [4096, 4096], P('dp', 'tensor'), may hold values from -0.11328125 to 0.11328125
- w_key: bfloat16 [4096, 1024], P('dp', 'tensor'), may hold values from -0.11328125 to 0.11328125
- w_value: bfloat16 [4096, 1024], P('dp', 'tensor'), may hold values from -0.09375 to 0.09375
- w_out: bfloat16 [4096, 4096], P('tensor', 'dp'), may hold values from -0.09375 to 0.09375
- segment: int32 [4096], P('dp'), may hold values from -1 to 1, as said below
Outputs:
- hidden_out: bfloat16 [4096, 4096], P(('dp', 'tensor'))
- kv_cache: bfloat16 [4096, 8, 256], P('dp', 'tensor')
Inputs may be any that keep to these rules, and one draw needn't show every extreme that they name: `segment`: within each pack of 256 rows, prompts are numbered from 0 in order and each starts at a multiple of 128; a prompt's last tile may end in rows of -1, and whole tiles of -1 may only follow the last prompt of a pack; the first tile of every pack holds a prompt; in every draw some pack has no tile of -1 only and holds one prompt a tile.
All inputs are finite; a program needn't handle non-finite values.
Results may differ from a plain program's by a relative error of at most 0.0085.
Values may be sent and summed in bfloat16 or wider, within the bound.
A program may use at most 128 MiB of HBM per device.

v0:
```python
import functools

import jax
import jax.numpy as jnp
from jax import lax
from jax.experimental import pallas as pl
from jax.experimental.pallas import tpu as pltpu
from jax.sharding import PartitionSpec as P

HEAD = 128


rope_theta = 500000.0
norm_epsilon = 1e-05


def inverse_frequency(head_width):
    exponent = jnp.arange(0, head_width, 2).astype(jnp.float32) / head_width
    base_freq = rope_theta ** (-exponent)
    wavelength = 2.0 * jnp.pi / base_freq
    smooth = (8192.0 / wavelength - 1.0) / 3.0
    blended = (1.0 - smooth) * base_freq / 8.0 + smooth * base_freq
    return jnp.where(
        wavelength < 2048.0, base_freq, jnp.where(wavelength > 8192.0, base_freq / 8.0, blended)
    )


def positions_of(segment):
    row_index = jnp.arange(segment.shape[0], dtype=jnp.int32)
    changed = jnp.concatenate([jnp.ones((1,), dtype=bool), segment[1:] != segment[:-1]])
    earlier = changed[None, :] & (row_index[None, :] <= row_index[:, None])
    return row_index - jnp.max(jnp.where(earlier, row_index[None, :], 0), axis=1)


def rotate(vectors, position):
    head_width = vectors.shape[-1]
    half_width = head_width // 2
    angles = position.astype(jnp.float32)[:, None] * inverse_frequency(head_width)[None, :]
    cosine = jnp.concatenate([jnp.cos(angles), jnp.cos(angles)], axis=-1)[:, None, :]
    sine_table = jnp.concatenate([jnp.sin(angles), jnp.sin(angles)], axis=-1)[:, None, :]
    turned = jnp.concatenate([-vectors[..., half_width:], vectors[..., :half_width]], axis=-1)
    return vectors * cosine + turned * sine_table


def rms_normed(rows_float, norm_gain):
    mean_square = jnp.mean(rows_float * rows_float, axis=-1, keepdims=True)
    return (
        rows_float * lax.rsqrt(mean_square + norm_epsilon) * norm_gain.astype(jnp.float32)
    ).astype(jnp.bfloat16)


def visible_pairs(segment, key_count):
    row_index = jnp.arange(segment.shape[0], dtype=jnp.int32)
    key_index = jnp.arange(key_count, dtype=jnp.int32)
    same_segment = (segment[:, None] == segment[None, :]) & (segment[:, None] >= 0)
    causal = key_index[None, :] <= row_index[:, None]
    return same_segment & causal | (key_index[None, :] == row_index[:, None])


def body(hidden_in, norm_gain, w_query, w_key, w_value, w_out, segment):
    pack_rows = segment.shape[0]
    query_cols = w_query.shape[1]
    kv_cols = w_key.shape[1]
    query_heads = query_cols // HEAD
    kv_heads = kv_cols // HEAD
    group_size = query_heads // kv_heads
    score_scale = HEAD ** (-0.5)
    rows_float = hidden_in.astype(jnp.float32)
    normed = rms_normed(rows_float, norm_gain)
    gathered = lax.all_gather(normed, "tensor", axis=0, tiled=True)
    joined = jnp.concatenate(
        (
            lax.all_gather(w_query, "dp", axis=0, tiled=True),
            lax.all_gather(w_key, "dp", axis=0, tiled=True),
            lax.all_gather(w_value, "dp", axis=0, tiled=True),
        ),
        axis=1,
    )
    projected = jnp.dot(gathered, joined, preferred_element_type=jnp.float32)
    position = positions_of(segment)
    query_rows = rotate(
        projected[:, :query_cols].reshape(pack_rows, query_heads, HEAD), position
    ).astype(jnp.bfloat16)
    key_rows = rotate(
        projected[:, query_cols : query_cols + kv_cols].reshape(pack_rows, kv_heads, HEAD), position
    ).astype(jnp.bfloat16)
    value_rows = (
        projected[:, query_cols + kv_cols :].astype(jnp.bfloat16).reshape(pack_rows, kv_heads, HEAD)
    )
    cache_rows = jnp.concatenate([key_rows, value_rows], axis=-1)
    grouped_query = query_rows.reshape(pack_rows, kv_heads, group_size, HEAD)
    scores = (
        jnp.einsum("skgh,tkh->kgst", grouped_query, key_rows, preferred_element_type=jnp.float32)
        * score_scale
    )
    allowed = visible_pairs(segment, pack_rows)
    scores = jnp.where(allowed, scores, -1e30)
    row_max = jnp.max(scores, axis=-1, keepdims=True)
    weight = jnp.exp(scores - row_max)
    weight_sum = jnp.sum(weight, axis=-1)
    mixed_rows = (
        jnp.einsum(
            "kgst,tkh->kgsh",
            weight.astype(jnp.bfloat16),
            value_rows,
            preferred_element_type=jnp.float32,
        )
        / weight_sum[..., None]
    )
    attended = (
        jnp.transpose(mixed_rows, (2, 0, 1, 3)).astype(jnp.bfloat16).reshape(pack_rows, query_cols)
    )
    out_full = lax.all_gather(w_out, "dp", axis=1, tiled=True)
    summed = lax.psum_scatter(
        jnp.dot(attended, out_full, preferred_element_type=jnp.float32).astype(jnp.bfloat16),
        "tensor",
        scatter_dimension=0,
        tiled=True,
    ).astype(jnp.float32)
    hidden_out = (summed + rows_float).astype(jnp.bfloat16)
    return (hidden_out, cache_rows)


MESH = pl.DeviceIdType.MESH


def fused_kernel(
    nz, hidden_ref, gain_ref, wj_ref, wo_ref, aux_ref,
    out_ref, cache_ref,
    act, w_buf, o_buf, aux_buf, acc, att, part, got, cache_send, cache_got,
    local_sem, x_send, x_recv, act_send, act_recv,
    w_send, w_recv, o_send, o_recv, sum_send, sum_recv,
):
    dp = lax.axis_index("dp")
    y = lax.axis_index("tensor")
    z = dp // 4
    x = (dp // 2) % 2
    c = dp % 2
    ox, oy, oc = 1 - x, 1 - y, 1 - c

    def dev(zz, xx, cc, yy):
        return {"dp": zz * 4 + xx * 2 + cc, "tensor": yy}

    x_peer = dev(z, ox, c, y)
    sibling = dev(z, x, oc, y)
    has_up = z + 1 < nz
    has_down = z > 0
    up = dev(jnp.minimum(z + 1, nz - 1), x, c, y)
    down = dev(jnp.maximum(z - 1, 0), x, c, y)
    trio = ((0, 1), (1, 0), (1, 1))

    def flip(delta):
        return (x + delta[0]) % 2, (y + delta[1]) % 2

    barrier = pltpu.get_barrier_semaphore()
    for delta in trio:
        px, py = flip(delta)
        pl.semaphore_signal(barrier, inc=1, device_id=dev(z, px, c, py), device_id_type=MESH)
    pl.semaphore_signal(barrier, inc=1, device_id=sibling, device_id_type=MESH)

    @pl.when(has_up)
    def _():
        pl.semaphore_signal(barrier, inc=1, device_id=up, device_id_type=MESH)

    @pl.when(has_down)
    def _():
        pl.semaphore_signal(barrier, inc=1, device_id=down, device_id_type=MESH)

    pl.semaphore_wait(barrier, 4 + jnp.where(has_up, 1, 0) + jnp.where(has_down, 1, 0))

    def remote(src, dst, send, recv, device):
        return pltpu.make_async_remote_copy(
            src_ref=src, dst_ref=dst, send_sem=send, recv_sem=recv, device_id=device, device_id_type=MESH
        )

    class Ring:
        def __init__(self, buf, src, send, recv, at):
            self.buf, self.src, self.send, self.recv, self.at = buf, src, send, recv, at

        def own(self, h):
            return pltpu.make_async_copy(
                self.src.at[x, h], self.buf.at[z, x, c, h], local_sem.at[self.at + h]
            )

        def cross(self, h):
            return remote(
                self.src.at[ox, h], self.buf.at[z, x, c, h],
                x_send.at[self.at + h], self.recv.at[z, x, c, h], x_peer,
            )

        def hop(self, way, zs, xs, h, device):
            slot = self.buf.at[zs, xs, c, h]
            return remote(slot, slot, self.send.at[way, zs, xs, h], self.recv.at[zs, xs, c, h], device)

        def arrived(self, zs, xs, cc, h):
            slot = self.buf.at[zs, xs, cc, h]
            remote(slot, slot, self.send.at[0, 0, 0, 0], self.recv.at[zs, xs, cc, h], sibling).wait_recv()

        def forward(self, d, work=None, first=0, last=4):
            def one(t, carry):
                xs = (x + t // 2) % 2
                h = t % 2
                if d == 0:
                    @pl.when(t >= 2)
                    def _():
                        self.arrived(z, xs, c, h)

                    @pl.when(has_up)
                    def _():
                        self.hop(0, z, xs, h, up).start()

                    @pl.when(has_down)
                    def _():
                        self.hop(1, z, xs, h, down).start()

                    self.hop(2, z, xs, h, sibling).start()
                else:
                    @pl.when(z - d >= 0)
                    def _():
                        zs = z - d
                        self.arrived(zs, xs, c, h)

                        @pl.when(has_up)
                        def _():
                            self.hop(0, zs, xs, h, up).start()

                        self.hop(2, zs, xs, h, sibling).start()

                    @pl.when(z + d < nz)
                    def _():
                        zs = z + d
                        self.arrived(zs, xs, c, h)

                        @pl.when(has_down)
                        def _():
                            self.hop(1, zs, xs, h, down).start()

                        self.hop(2, zs, xs, h, sibling).start()

                if work is not None:
                    work(t)
                return carry

            lax.fori_loop(first, last, one, 0)

        def sibling_part(self, zs):
            def one(t, carry):
                self.arrived(zs, (x + t // 2) % 2, oc, t % 2)
                return carry

            lax.fori_loop(0, 4, one, 0)

        def finish(self):
            for h in range(2):
                self.cross(h).wait_send()

            def one(t, carry):
                zs, xs, h = t // 4, (t // 2) % 2, t % 2

                @pl.when((zs <= z) & has_up)
                def _():
                    self.hop(0, zs, xs, h, up).wait_send()

                @pl.when((zs >= z) & has_down)
                def _():
                    self.hop(1, zs, xs, h, down).wait_send()

                self.hop(2, zs, xs, h, sibling).wait_send()
                return carry

            lax.fori_loop(0, nz * 4, one, 0)

    qkv = Ring(w_buf, wj_ref, w_send, w_recv, 0)
    outw = Ring(o_buf, wo_ref, o_send, o_recv, 2)

    for h in range(2):
        qkv.cross(h).start()
    for ring in (qkv, outw):
        for h in range(2):
            ring.own(h).start()
    for h in range(2):
        qkv.own(h).wait()
    qkv.forward(0, last=2)

    rows = hidden_ref[...].astype(jnp.float32)
    mean_square = jnp.mean(rows * rows, axis=-1, keepdims=True)
    mine = x * 2 + y
    act[mine] = (rows * lax.rsqrt(mean_square + norm_epsilon) * gain_ref[...]).astype(jnp.bfloat16)
    aux_buf[x] = aux_ref[...]

    def act_copy(k):
        px, py = flip(trio[k])
        return remote(act.at[mine], act.at[mine], act_send.at[k], act_recv.at[mine], dev(z, px, c, py))

    for k in range(3):
        act_copy(k).start()
    aux_copy = remote(aux_ref, aux_buf.at[x], x_send.at[4], x_recv.at[0], x_peer)
    aux_copy.start()
    qkv.forward(0, first=2)
    for h in range(2):
        outw.own(h).wait()

    rows_here = act.shape[0] * act.shape[1]
    span = act.shape[2] // nz
    width = acc.shape[1]
    acc[...] = jnp.zeros_like(acc)

    chunks = width // 256

    def project(zs, t):
        cols = pl.ds(pl.multiple_of(zs * span, span), span)

        def one(n, carry):
            at = pl.ds(pl.multiple_of(n * 256, 256), 256)
            left = act[:, :, cols].reshape(rows_here, span)
            right = w_buf[zs, :, :, :, :, at].reshape(span, 256)
            acc[:, at] += jnp.dot(left, right, preferred_element_type=jnp.float32)
            return carry

        @pl.when(t == 0)
        def _():
            qkv.sibling_part(zs)

        lax.fori_loop(t * chunks // 4, (t + 1) * chunks // 4, one, 0)

    def each(d, work):
        if d == 0:
            work(z)
        else:
            @pl.when(z - d >= 0)
            def _():
                work(z - d)

            @pl.when(z + d < nz)
            def _():
                work(z + d)

    def part_of(d, work):
        return lambda t: each(d, lambda zs: work(zs, t))

    def whole_of(d, work):
        def one(t, carry):
            part_of(d, work)(t)
            return carry

        lax.fori_loop(0, 4, one, 0)

    qkv.forward(1)
    for k in range(3):
        px, py = flip(trio[k])
        q = px * 2 + py
        remote(act.at[q], act.at[q], act_send.at[0], act_recv.at[q], sibling).wait_recv()
    for h in range(2):
        outw.cross(h).start()
    for d in range(2, nz):
        qkv.forward(d, part_of(d - 2, project))
    outw.forward(0)
    for d in range(nz - 2, nz):
        whole_of(d, project)

    aux_copy.wait_send()
    remote(aux_ref, aux_buf.at[ox], x_send.at[4], x_recv.at[0], x_peer).wait_recv()
    lane = lax.broadcasted_iota(jnp.int32, (256, HEAD), 1)
    row_at = lax.broadcasted_iota(jnp.int32, (256, 256), 0)
    key_at = lax.broadcasted_iota(jnp.int32, (256, 256), 1)
    query_width = att.shape[1]
    kv_heads = (width - query_width) // (2 * HEAD)
    group = query_width // HEAD // kv_heads

    def attend(t):
        p = (ox + t // kv_heads) % 2
        g = t % kv_heads
        table = aux_buf[p, 0:256, :]
        swapped = pltpu.roll(table, HEAD // 2, 1)
        cosine = jnp.where(lane < HEAD // 2, table, swapped)
        sine = jnp.where(lane < HEAD // 2, -swapped, table)
        seg = jnp.concatenate([aux_buf[p, 256:257, :], aux_buf[p, 257:258, :]], axis=1)
        seg_key = jnp.broadcast_to(seg, (256, 256))
        seg_row = seg_key.T
        allowed = ((seg_key == seg_row) & (seg_row >= 0) & (key_at <= row_at)) | (key_at == row_at)
        pack = pl.ds(pl.multiple_of(p * 256, 256), 256)

        def head_of(at):
            return acc[pack, pl.ds(pl.multiple_of(at * HEAD, HEAD), HEAD)]

        def turned(v):
            return (v * cosine + pltpu.roll(v, HEAD // 2, 1) * sine).astype(jnp.bfloat16)

        key = turned(head_of(query_width // HEAD + g))
        value = head_of(query_width // HEAD + kv_heads + g).astype(jnp.bfloat16)
        cache_send[p, :, pl.ds(pl.multiple_of(g * 256, 256), HEAD)] = key
        cache_send[p, :, pl.ds(pl.multiple_of(g * 256 + HEAD, HEAD), HEAD)] = value
        for i in range(group):
            query = turned(head_of(g * group + i))
            scores = lax.dot_general(
                query, key, (((1,), (1,)), ((), ())), preferred_element_type=jnp.float32
            ) * HEAD ** (-0.5)
            scores = jnp.where(allowed, scores, -1e30)
            weight = jnp.exp(scores - jnp.max(scores, axis=-1, keepdims=True))
            total = jnp.sum(weight, axis=-1, keepdims=True)
            mixed = jnp.dot(weight.astype(jnp.bfloat16), value, preferred_element_type=jnp.float32)
            att[pack, pl.ds(pl.multiple_of((g * group + i) * HEAD, HEAD), HEAD)] = (mixed / total).astype(
                jnp.bfloat16
            )

    outw.forward(1, attend)
    cache_copy = remote(cache_send.at[ox], cache_got, x_send.at[5], x_recv.at[1], x_peer)
    cache_copy.start()

    depth, cols_out = o_buf.shape[3] * o_buf.shape[4], o_buf.shape[5]

    def strip(n):
        return pl.ds(pl.multiple_of(n * cols_out, cols_out), cols_out)

    def sum_copy(zs, n, k):
        px, py = flip(trio[k])
        return remote(
            part.at[zs, px * 2 + py, :, strip(n)], got.at[zs, k, :, strip(n)],
            sum_send.at[zs, n, k], sum_recv.at[zs, n, k], dev(z, px, c, py),
        )

    def outward(zs, n):
        xs, cs = n // 2, n % 2

        @pl.when(cs == oc)
        def _():
            for h in range(2):
                outw.arrived(zs, xs, oc, h)

        right = o_buf[zs, xs, cs].reshape(depth, cols_out)
        product = jnp.dot(att[...], right, preferred_element_type=jnp.float32)
        part[zs, :, :, strip(n)] = product.astype(jnp.bfloat16).reshape(4, rows_here // 4, cols_out)
        for k in (2, 1, 0):
            sum_copy(zs, n, k).start()

    for d in range(2, nz):
        early = part_of(d - 2, outward)
        if d < nz - 1:
            outw.forward(d, early)
        else:
            late = part_of(d - 1, outward)

            def both(t):
                early(t)
                late(t)

            outw.forward(d, both)
    whole_of(nz - 1, outward)

    cache_copy.wait()
    kept = cache_ref.shape[1] // 2
    cache_ref[:, pl.ds(pl.multiple_of(x * kept, kept), kept)] = cache_send[x]
    cache_ref[:, pl.ds(pl.multiple_of(ox * kept, kept), kept)] = cache_got[...]
    qkv.finish()
    outw.finish()
    for k in range(3):
        act_copy(k).wait_send()

    def settle(zs):
        for n in range(4):
            for k in range(3):
                sum_copy(zs, n, k).wait()
        cols = pl.ds(pl.multiple_of(zs * span, span), span)
        total = part[zs, mine].astype(jnp.float32)
        for k in range(3):
            total = total + got[zs, k].astype(jnp.float32)
        out_ref[:, cols] = (total + hidden_ref[:, cols].astype(jnp.float32)).astype(jnp.bfloat16)

    for d in range(nz):
        each(d, settle)


def fused_body(n_dp, hidden_in, norm_gain, w_query, w_key, w_value, w_out, segment):
    nz = n_dp // 4
    rows, features = hidden_in.shape
    pack_rows = segment.shape[0]
    depth, query_cols = w_query.shape
    kv_cols = w_key.shape[1]
    width = (query_cols + 2 * kv_cols) // 2
    out_cols = w_out.shape[1]

    def halves(w):
        return jnp.transpose(w.reshape(depth, 2, w.shape[1] // 2), (1, 0, 2))

    joined = jnp.concatenate((halves(w_query), halves(w_key), halves(w_value)), axis=2)
    joined = joined.reshape(2, 2, depth // 2, width)
    out_parts = w_out.reshape(2, 2, query_cols // 4, out_cols)
    angles = positions_of(segment).astype(jnp.float32)[:, None] * inverse_frequency(HEAD)[None, :]
    aux = jnp.concatenate(
        (
            jnp.cos(angles), jnp.sin(angles),
        ),
        axis=1,
    )
    aux = jnp.concatenate(
        (aux, segment.astype(jnp.float32).reshape(pack_rows // 128, 128), jnp.zeros((6, 128), jnp.float32)), axis=0
    )
    vmem = pl.BlockSpec(memory_space=pltpu.VMEM)
    dma = pltpu.SemaphoreType.DMA
    low = jnp.bfloat16
    hidden_out, cache = pl.pallas_call(
        functools.partial(fused_kernel, nz),
        out_shape=(
            jax.ShapeDtypeStruct((rows, features), low),
            jax.ShapeDtypeStruct((pack_rows, 2 * kv_cols), low),
        ),
        in_specs=[vmem] * 5,
        out_specs=(vmem, vmem),
        scratch_shapes=[
            pltpu.VMEM((4, rows, features), low),
            pltpu.VMEM((nz, 2, 2, 2, depth // 2, width), low),
            pltpu.VMEM((nz, 2, 2, 2, query_cols // 4, out_cols), low),
            pltpu.VMEM((2,) + aux.shape, jnp.float32),
            pltpu.VMEM((4 * rows, width), jnp.float32),
            pltpu.VMEM((4 * rows, query_cols // 2), low),
            pltpu.VMEM((nz, 4, rows, features // nz), low),
            pltpu.VMEM((nz, 3, rows, features // nz), low),
            pltpu.VMEM((2, pack_rows, kv_cols), low),
            pltpu.VMEM((pack_rows, kv_cols), low),
            dma((4,)), dma((6,)), dma((2,)), dma((3,)), dma((4,)),
            dma((3, nz, 2, 2)), dma((nz, 2, 2, 2)), dma((3, nz, 2, 2)), dma((nz, 2, 2, 2)),
            dma((nz, 4, 3)), dma((nz, 4, 3)),
        ],
        compiler_params=pltpu.CompilerParams(
            collective_id=0, has_side_effects=True, vmem_limit_bytes=60 * 1024 * 1024
        ),
    )(hidden_in, norm_gain.astype(jnp.float32).reshape(1, features), joined, out_parts, aux)
    return hidden_out, cache.reshape(pack_rows, kv_cols // HEAD, 2 * HEAD)


def solution(mesh):
    n_dp, n_tensor = mesh.shape["dp"], mesh.shape["tensor"]

    def chosen(*blocks):
        if n_tensor == 2 and n_dp % 4 == 0 and n_dp >= 12 and blocks[3].shape[1] == 4 * HEAD:
            return fused_body(n_dp, *blocks)
        return body(*blocks)

    return jax.shard_map(
        chosen,
        mesh=mesh,
        in_specs=(
            P(("dp", "tensor"), None),
            P(),
            P("dp", "tensor"),
            P("dp", "tensor"),
            P("dp", "tensor"),
            P("tensor", "dp"),
            P("dp"),
        ),
        out_specs=(P(("dp", "tensor"), None), P("dp", "tensor", None)),
        check_vma=False,
    )
```

profile of v0, /device:TPU:0, one launch (start us, length us, event | category | flops | bytes accessed | tf_op | source)
XLA Modules:
  0.0 209.7 jit_solution(1078461481412046127)
XLA Ops:
  0.6 0.0 copy-start
  0.6 0.9 slice_compare_fusion
  1.5 0.1 pad_add_fusion
  1.6 0.1 select_reduce_fusion
  1.7 0.7 convert_bitcast_fusion
  2.4 0.1 pad.3.clone
  2.5 1.3 reshape.70
  3.8 0.5 multiply_cosine_fusion
  4.3 0.8 maximum_maximum_fusion.aux_ref
  5.1 1.1 bitcast_bitcast_fusion.1
  6.2 0.0 copy-done
  6.2 0.1 copy.21
  6.3 1.3 pad_maximum_fusion
  7.6 198.8 %shard_map.86 = (bf16[128,4096]{1,0:T(8,128)(2,1)}, bf16[256,1024]{1,0:T(8,128)(2,1)}) custom-call(bf16[128,4096]{1,0:T(8,128)(2,1)} %hidden_ref.1, f32[1,4096]{1,0:T(1,128)} %bitcast.28, bf16[2,2,128,1536]{3,2,1,0:T(8,128)(2,1)} %bitcast.22, bf16[2,2,512,256]{3,2,1,0:T(8,128)(2,1)} %bitcast.24, f32[264,128]{1,0:T(8,128)} %maximum_maximum_fusion.aux_ref), custom_call_target="tpu_custom_call" | custom-call | tf_op jit(solution)/shard_map/pallas_call | solution.py:501
  206.4 0.0 copy-start.1
  206.4 2.3 %reshape.69 = bf16[256,4,256]{2,1,0:T(4,128)(2,1)} reshape(bf16[256,1024]{1,0:T(8,128)(2,1)} %get-tuple-element.5) | data formatting | bytes 1048576 | tf_op jit(solution)/shard_map/reshape | solution.py:528
  208.7 0.0 copy-done.1
  208.7 1.0 copy.23
  (3 shorter events, 0.0 us)
Async XLA Ops:
  0.6 5.6 %copy-start = (bf16[256,2048]{1,0:T(8,128)(2,1)S(1)}, bf16[256,2048]{1,0:T(8,128)(2,1)}, u32[]{:S(2)}) copy-start(bf16[256,2048]{1,0:T(8,128)(2,1)} %param.9) | copy-start | bytes 3145732
  206.4 2.3 %copy-start.1 = (bf16[128,4096]{1,0:T(8,128)(2,1)S(1)}, bf16[128,4096]{1,0:T(8,128)(2,1)}, u32[]{:S(2)}) copy-start(bf16[128,4096]{1,0:T(8,128)(2,1)} %get-tuple-element.12) | copy-start | bytes 3145732
where the time goes:
time: 210 us
  Pallas kernels  199 us (95%)
  other arithmetic  5.69 us (3%)
  local copies, waits for them, and re-layouts  4.51 us (2%)
    pallas_call x1, Pallas kernels, fused_body(): pl.pallas_call(functools.partial(fused_kernel, nz), out_shape=(jax.ShapeD...  199 us

commit v1 on v0

--- a/solution.py
+++ b/solution.py
@@ -433,6 +433,9 @@
         for k in (2, 1, 0):
             sum_copy(zs, n, k).start()
 
+    def final_strip(zs, k):
+        outward(zs, (x + k // 2) % 2 * 2 + (c + k % 2) % 2)
+
     for d in range(2, nz):
         early = part_of(d - 2, outward)
         if d < nz - 1:
@@ -444,8 +447,12 @@
                 early(t)
                 late(t)
 
+                @pl.when(t > 0)
+                def _():
+                    each(d, lambda zs: final_strip(zs, t - 1))
+
             outw.forward(d, both)
-    whole_of(nz - 1, outward)
+    each(nz - 1, lambda zs: final_strip(zs, 3))
 
     cache_copy.wait()
     kept = cache_ref.shape[1] // 2

time: 210 us -> 210 us (level)
  no operation moved by 1% of the time
where the time goes in v1:
time: 210 us
  Pallas kernels  199 us (95%)
  other arithmetic  5.69 us (3%)
  local copies, waits for them, and re-layouts  4.51 us (2%)
    pallas_call x1, Pallas kernels, fused_body(): pl.pallas_call(functools.partial(fused_kernel, nz), out_shape=(jax.ShapeD...  199 us

profile of v1, /device:TPU:0, one launch (start us, length us, event | category | flops | bytes accessed | tf_op | source)
XLA Modules:
  0.0 210.0 jit_solution(7900781949546642852)
XLA Ops:
  0.6 0.0 copy-start
  0.6 0.9 slice_compare_fusion
  1.5 0.1 pad_add_fusion
  1.6 0.1 select_reduce_fusion
  1.7 0.7 convert_bitcast_fusion
  2.4 0.1 pad.3.clone
  2.5 1.3 reshape.70
  3.8 0.5 multiply_cosine_fusion
  4.3 0.8 maximum_maximum_fusion.aux_ref
  5.1 1.1 bitcast_bitcast_fusion.1
  6.2 0.0 copy-done
  6.2 0.1 copy.21
  6.3 1.3 pad_maximum_fusion
  7.6 199.1 %shard_map.86 = (bf16[128,4096]{1,0:T(8,128)(2,1)}, bf16[256,1024]{1,0:T(8,128)(2,1)}) custom-call(bf16[128,4096]{1,0:T(8,128)(2,1)} %hidden_ref.1, f32[1,4096]{1,0:T(1,128)} %bitcast.28, bf16[2,2,128,1536]{3,2,1,0:T(8,128)(2,1)} %bitcast.22, bf16[2,2,512,256]{3,2,1,0:T(8,128)(2,1)} %bitcast.24, f32[264,128]{1,0:T(8,128)} %maximum_maximum_fusion.aux_ref), custom_call_target="tpu_custom_call" | custom-call | tf_op jit(solution)/shard_map/pallas_call | solution.py:508
  206.7 0.0 copy-start.1
  206.7 2.3 %reshape.69 = bf16[256,4,256]{2,1,0:T(4,128)(2,1)} reshape(bf16[256,1024]{1,0:T(8,128)(2,1)} %get-tuple-element.5) | data formatting | bytes 1048576 | tf_op jit(solution)/shard_map/reshape | solution.py:535
  209.0 0.0 copy-done.1
  209.0 1.0 copy.23
  (3 shorter events, 0.0 us)
Async XLA Ops:
  0.6 5.6 %copy-start = (bf16[256,2048]{1,0:T(8,128)(2,1)S(1)}, bf16[256,2048]{1,0:T(8,128)(2,1)}, u32[]{:S(2)}) copy-start(bf16[256,2048]{1,0:T(8,128)(2,1)} %param.9) | copy-start | bytes 3145732
  206.7 2.3 %copy-start.1 = (bf16[128,4096]{1,0:T(8,128)(2,1)S(1)}, bf16[128,4096]{1,0:T(8,128)(2,1)}, u32[]{:S(2)}) copy-start(bf16[128,4096]{1,0:T(8,128)(2,1)} %get-tuple-element.12) | copy-start | bytes 3145732

commit v2 on v1

--- a/solution.py
+++ b/solution.py
@@ -125,7 +125,7 @@
 
 
 def fused_kernel(
-    nz, hidden_ref, gain_ref, wj_ref, wo_ref, aux_ref,
+    nz, hidden_ref, gain_ref, wq_ref, wk_ref, wv_ref, wo_ref, aux_ref,
     out_ref, cache_ref,
     act, w_buf, o_buf, aux_buf, acc, att, part, got, cache_send, cache_got,
     local_sem, x_send, x_recv, act_send, act_recv,
@@ -177,16 +177,32 @@
         def __init__(self, buf, src, send, recv, at):
             self.buf, self.src, self.send, self.recv, self.at = buf, src, send, recv, at
 
+        def pieces(self, xx, h):
+            slot = self.buf.at[z, x, c, h]
+            if len(self.src) == 1:
+                return [(self.src[0].at[xx, h], slot)]
+            found, start = [], 0
+            for ref in self.src:
+                tall, wide = ref.shape[0] // 2, ref.shape[1] // 2
+                cols = pl.ds(pl.multiple_of(xx * wide, wide), wide)
+                found.append(
+                    (ref.at[pl.ds(h * tall, tall), cols], self.buf.at[z, x, c, h, :, pl.ds(start, wide)])
+                )
+                start += wide
+            return found
+
         def own(self, h):
-            return pltpu.make_async_copy(
-                self.src.at[x, h], self.buf.at[z, x, c, h], local_sem.at[self.at + h]
-            )
+            found = self.pieces(x, h)
+            at = self.at + h * len(found)
+            return [pltpu.make_async_copy(a, b, local_sem.at[at + i]) for i, (a, b) in enumerate(found)]
 
         def cross(self, h):
-            return remote(
-                self.src.at[ox, h], self.buf.at[z, x, c, h],
-                x_send.at[self.at + h], self.recv.at[z, x, c, h], x_peer,
-            )
+            found = self.pieces(ox, h)
+            at = self.at + h * len(found)
+            return [
+                remote(a, b, x_send.at[at + i], self.recv.at[z, x, c, h], x_peer)
+                for i, (a, b) in enumerate(found)
+            ]
 
         def hop(self, way, zs, xs, h, device):
             slot = self.buf.at[zs, xs, c, h]
@@ -252,7 +268,8 @@
 
         def finish(self):
             for h in range(2):
-                self.cross(h).wait_send()
+                for copy in self.cross(h):
+                    copy.wait_send()
 
             def one(t, carry):
                 zs, xs, h = t // 4, (t // 2) % 2, t % 2
@@ -270,16 +287,19 @@
 
             lax.fori_loop(0, nz * 4, one, 0)
 
-    qkv = Ring(w_buf, wj_ref, w_send, w_recv, 0)
-    outw = Ring(o_buf, wo_ref, o_send, o_recv, 2)
+    qkv = Ring(w_buf, (wq_ref, wk_ref, wv_ref), w_send, w_recv, 0)
+    outw = Ring(o_buf, (wo_ref,), o_send, o_recv, 6)
 
     for h in range(2):
-        qkv.cross(h).start()
+        for copy in qkv.cross(h):
+            copy.start()
     for ring in (qkv, outw):
         for h in range(2):
-            ring.own(h).start()
+            for copy in ring.own(h):
+                copy.start()
     for h in range(2):
-        qkv.own(h).wait()
+        for copy in qkv.own(h):
+            copy.wait()
     qkv.forward(0, last=2)
 
     rows = hidden_ref[...].astype(jnp.float32)
@@ -294,11 +314,12 @@
 
     for k in range(3):
         act_copy(k).start()
-    aux_copy = remote(aux_ref, aux_buf.at[x], x_send.at[4], x_recv.at[0], x_peer)
+    aux_copy = remote(aux_ref, aux_buf.at[x], x_send.at[8], x_recv.at[0], x_peer)
     aux_copy.start()
     qkv.forward(0, first=2)
     for h in range(2):
-        outw.own(h).wait()
+        for copy in outw.own(h):
+            copy.wait()
 
     rows_here = act.shape[0] * act.shape[1]
     span = act.shape[2] // nz
@@ -351,7 +372,8 @@
         q = px * 2 + py
         remote(act.at[q], act.at[q], act_send.at[0], act_recv.at[q], sibling).wait_recv()
     for h in range(2):
-        outw.cross(h).start()
+        for copy in outw.cross(h):
+            copy.start()
     for d in range(2, nz):
         qkv.forward(d, part_of(d - 2, project))
     outw.forward(0)
@@ -359,7 +381,7 @@
         whole_of(d, project)
 
     aux_copy.wait_send()
-    remote(aux_ref, aux_buf.at[ox], x_send.at[4], x_recv.at[0], x_peer).wait_recv()
+    remote(aux_ref, aux_buf.at[ox], x_send.at[8], x_recv.at[0], x_peer).wait_recv()
     lane = lax.broadcasted_iota(jnp.int32, (256, HEAD), 1)
     row_at = lax.broadcasted_iota(jnp.int32, (256, 256), 0)
     key_at = lax.broadcasted_iota(jnp.int32, (256, 256), 1)
@@ -404,7 +426,7 @@
             )
 
     outw.forward(1, attend)
-    cache_copy = remote(cache_send.at[ox], cache_got, x_send.at[5], x_recv.at[1], x_peer)
+    cache_copy = remote(cache_send.at[ox], cache_got, x_send.at[9], x_recv.at[1], x_peer)
     cache_copy.start()
 
     depth, cols_out = o_buf.shape[3] * o_buf.shape[4], o_buf.shape[5]
@@ -486,11 +508,6 @@
     width = (query_cols + 2 * kv_cols) // 2
     out_cols = w_out.shape[1]
 
-    def halves(w):
-        return jnp.transpose(w.reshape(depth, 2, w.shape[1] // 2), (1, 0, 2))
-
-    joined = jnp.concatenate((halves(w_query), halves(w_key), halves(w_value)), axis=2)
-    joined = joined.reshape(2, 2, depth // 2, width)
     out_parts = w_out.reshape(2, 2, query_cols // 4, out_cols)
     angles = positions_of(segment).astype(jnp.float32)[:, None] * inverse_frequency(HEAD)[None, :]
     aux = jnp.concatenate(
@@ -511,7 +528,7 @@
             jax.ShapeDtypeStruct((rows, features), low),
             jax.ShapeDtypeStruct((pack_rows, 2 * kv_cols), low),
         ),
-        in_specs=[vmem] * 5,
+        in_specs=[vmem] * 7,
         out_specs=(vmem, vmem),
         scratch_shapes=[
             pltpu.VMEM((4, rows, features), low),
@@ -524,14 +541,14 @@
             pltpu.VMEM((nz, 3, rows, features // nz), low),
             pltpu.VMEM((2, pack_rows, kv_cols), low),
             pltpu.VMEM((pack_rows, kv_cols), low),
-            dma((4,)), dma((6,)), dma((2,)), dma((3,)), dma((4,)),
+            dma((8,)), dma((10,)), dma((2,)), dma((3,)), dma((4,)),
             dma((3, nz, 2, 2)), dma((nz, 2, 2, 2)), dma((3, nz, 2, 2)), dma((nz, 2, 2, 2)),
             dma((nz, 4, 3)), dma((nz, 4, 3)),
         ],
         compiler_params=pltpu.CompilerParams(
             collective_id=0, has_side_effects=True, vmem_limit_bytes=60 * 1024 * 1024
         ),
-    )(hidden_in, norm_gain.astype(jnp.float32).reshape(1, features), joined, out_parts, aux)
+    )(hidden_in, norm_gain.astype(jnp.float32).reshape(1, features), w_query, w_key, w_value, out_parts, aux)
     return hidden_out, cache.reshape(pack_rows, kv_cols // HEAD, 2 * HEAD)
 
 

time: 210 us -> 206 us (0.981)
  other arithmetic: 5.69 us -> 2.24 us
where the time goes in v2:
time: 206 us
  Pallas kernels  199 us (97%)
  local copies, waits for them, and re-layouts  4.33 us (2%)
  other arithmetic  2.24 us (1%)
    pallas_call x1, Pallas kernels, fused_body(): pl.pallas_call(functools.partial(fused_kernel, nz), out_shape=(jax.ShapeD...  199 us

profile of v2, /device:TPU:0, one launch (start us, length us, event | category | flops | bytes accessed | tf_op | source)
XLA Modules:
  0.0 206.1 jit_solution(5256993489934502050)
XLA Ops:
  0.6 0.0 copy-start.1
  0.6 0.7 copy-done.1
  1.3 0.0 copy-start.2
  1.3 0.1 slice_compare_fusion
  1.4 0.1 pad_add_fusion
  1.5 0.1 select_reduce_fusion
  1.6 0.1 pad.3.clone
  1.7 0.3 copy-done.2
  2.0 0.6 reshape.54
  2.6 0.5 multiply_cosine_fusion
  3.2 0.8 maximum_maximum_fusion.aux_ref
  3.9 198.9 %shard_map.86 = (bf16[128,4096]{1,0:T(8,128)(2,1)}, bf16[256,1024]{1,0:T(8,128)(2,1)}) custom-call(bf16[128,4096]{1,0:T(8,128)(2,1)} %hidden_ref.1, f32[1,4096]{1,0:T(1,128)} %bitcast.5, bf16[256,2048]{1,0:T(8,128)(2,1)} %wq_ref.1, bf16[256,512]{1,0:T(8,128)(2,1)} %wk_ref.1, bf16[256,512]{1,0:T(8,128)(2,1)} %wv_ref.1, bf16[2,2,512,256]{3,2,1,0:T(8,128)(2,1)} %bitcast.4, ...), custom_call_target="tpu_custom_call" | custom-call | tf_op jit(solution)/shard_map/pallas_call | solution.py:525
  202.8 0.0 copy-start
  202.8 2.3 %reshape.53 = bf16[256,4,256]{2,1,0:T(4,128)(2,1)} reshape(bf16[256,1024]{1,0:T(8,128)(2,1)} %get-tuple-element.5) | data formatting | bytes 1048576 | tf_op jit(solution)/shard_map/reshape | solution.py:552
  205.1 0.0 copy-done
  205.1 1.0 copy.10
  (4 shorter events, 0.0 us)
Async XLA Ops:
  0.6 0.7 copy-start.1
  1.3 0.7 copy-start.2
  202.8 2.3 %copy-start = (bf16[128,4096]{1,0:T(8,128)(2,1)S(1)}, bf16[128,4096]{1,0:T(8,128)(2,1)}, u32[]{:S(2)}) copy-start(bf16[128,4096]{1,0:T(8,128)(2,1)} %get-tuple-element.10) | copy-start | bytes 3145732
